TPU v7x, 128 devices: a whole 4x4x4 slice. The times are simulated.
128 devices in a mesh: segment: 2 (over y_lo), blk: 8 (over z, y_hi), rows: 8 (over x, core).
Axes of the slice: x: 4, y: 4 (y_hi: 2, y_lo: 2; y = y_hi * 2 + y_lo), z: 4, core: 2. Of those that a mesh axis runs over, the one named last changes fastest.
Arguments:
- nodal_disp: float32 [8, 3, 262144], P(None, None, ('blk', 'rows')), may hold values from -0.3 to 0.3
- connect: int32 [8, 262144], P(None, ('blk', 'rows')), may hold values from 0 to 4095
- brick_size: float32 [262144], P(('blk', 'rows')), may hold values from 0.5 to 2
- shear_modulus: float32 [262144], P(('blk', 'rows')), may hold values from 3 to 12
- bulk_modulus: float32 [262144], P(('blk', 'rows')), may hold values from 5 to 20
- cohesion: float32 [262144], P(('blk', 'rows')), may hold values from 0.3 to 3
- friction: float32 [262144], P(('blk', 'rows')), may hold values from 0.1 to 0.6
- active: int32 [262144], P(('blk', 'rows')), may hold values 0 or 1
- patch_brick: int32 [16384], P(('blk', 'rows')), may hold values from 0 to 4095
- patch_face: int32 [16384], P(('blk', 'rows')), may hold values from 0 to 5
- coords: float32 [3, 16384], P(None, ('blk', 'rows')), may hold values from -1 to 17, as said below
- radius: float32 [16384], P(('blk', 'rows')), may hold values from 0.03 to 0.0625
- stiffness: float32 [16384], P(('blk', 'rows')), may hold values from 0.1 to 0.3
Outputs:
- relaxed: float32 [8, 3, 16384], P(None, None, ('blk', 'rows'))
Inputs may be any that keep to these rules, and one draw needn't show every extreme that they name: `connect`: indexes the mesh nodes of the brick's own block. `patch_brick`: indexes the bricks of the node's own block. `patch_face`: 2 k for the plus face along dimension k, 2 k + 1 for the minus face. `coords`: collocation points on the slab.
All inputs are finite; a program needn't handle non-finite values. No bound on the sum of `active` on one device may be relied on, other than what follows from the above.
Results may differ from a plain program's by a relative error of at most 0.0004.
The roundings to bfloat16 on the way count: a program that leaves them out, or rounds other values in their place, can miss the bound.
Values may be sent and summed in bfloat16 or wider, within the bound.
A program may use at most 192 MiB of HBM per device.

v0:
```python
import math

import jax
import jax.numpy as jnp
from jax import lax
from jax.sharding import PartitionSpec as P

SWEEPS = 3


KELVIN_A = 1.0 / (1024.0 * math.pi)
KELVIN_B = KELVIN_A / 3.0
SMOOTH = 0.1
RELAXATION = 0.5


def from_behind(x, axis, by):
    length = lax.axis_size(axis)
    pairs = [(i, i + by) for i in range(length) if 0 <= i + by < length]
    return lax.ppermute(x, axis, pairs)


def corner_sign():
    corner = jnp.arange(8)
    powers = jnp.array([1, 2, 4])
    corner_bits = corner[:, None] // powers[None, :] % 2
    return (2 * corner_bits - 1).astype(jnp.float32)


def brick_stress(
    nodal_disp, connect, brick_size, shear_modulus, bulk_modulus, cohesion, friction, active
):
    signs_table = corner_sign()
    gradient = jnp.zeros((nodal_disp.shape[0], 3, 3, connect.shape[1]), jnp.float32)
    centre = jnp.zeros((nodal_disp.shape[0], 3, connect.shape[1]), jnp.float32)
    for corner in range(8):
        corner_disp = jnp.take(nodal_disp, connect[corner], axis=2)
        gradient = gradient + corner_disp[:, :, None, :] * signs_table[corner][None, None, :, None]
        centre = centre + corner_disp
    gradient = gradient / (4.0 * brick_size)
    centre = centre / 8.0
    strain = 0.5 * (gradient + jnp.swapaxes(gradient, 1, 2))
    volume = strain[:, 0, 0] + strain[:, 1, 1] + strain[:, 2, 2]
    identity = jnp.eye(3, dtype=jnp.float32)[None, :, :, None]
    pressure = bulk_modulus * volume
    deviator = 2.0 * shear_modulus * (strain - volume[:, None, None, :] / 3.0 * identity)
    second = 0.5 * jnp.sum(deviator * deviator, axis=(1, 2))
    scaling = jnp.maximum(cohesion - friction * pressure, SMOOTH) / jnp.sqrt(
        second + SMOOTH * SMOOTH
    )
    scaling = jnp.where(active == 1, scaling, 1.0)
    stress = scaling[:, None, None, :] * deviator + pressure[:, None, None, :] * identity
    return (stress, centre)


def interface(stress, centre, patch_brick, patch_face):
    picked = jnp.take(stress, patch_brick, axis=3)
    axis_of = patch_face // 2
    sign_of = (1 - 2 * (patch_face % 2)).astype(jnp.float32)
    normal = (jnp.arange(3)[:, None] == axis_of[None, :]).astype(jnp.float32) * sign_of[None, :]
    traction = jnp.sum(picked * normal[None, None, :, :], axis=2)
    fem_disp = jnp.take(centre, patch_brick, axis=2)
    return (traction.astype(jnp.bfloat16), fem_disp.astype(jnp.bfloat16))


def kelvin_tile(targets, points):
    offset = targets[:, :, None] - points[:3, None, :]
    spread = points[3]
    squared = jnp.sum(offset * offset, axis=0) + spread[None, :] * spread[None, :]
    inverse = lax.rsqrt(squared)
    inverse_cube = inverse * inverse * inverse
    diagonal = (KELVIN_A - KELVIN_B) * inverse + 0.5 * KELVIN_A * spread[None, :] * spread[
        None, :
    ] * inverse_cube
    identity = jnp.eye(3, dtype=jnp.float32)[:, :, None, None]
    kernel_tile = (
        identity * diagonal[None, None]
        + KELVIN_B * inverse_cube[None, None] * offset[:, None] * offset[None, :]
    )
    return kernel_tile.astype(jnp.bfloat16)


def apply_piece(targets, sources, density):
    width_all = density.shape[2]
    step_width = math.gcd(width_all, 256)

    def accumulate(running_sum, block_index):
        first_column = block_index * step_width
        points = lax.dynamic_slice_in_dim(sources, first_column, step_width, 1)
        block_density = lax.dynamic_slice_in_dim(density, block_index * step_width, step_width, 2)
        kernel_tile = kelvin_tile(targets, points)
        product = jnp.einsum(
            "mbk,abnk->man", block_density, kernel_tile, preferred_element_type=jnp.float32
        )
        return (running_sum + product, None)

    zeros_init = jnp.zeros((density.shape[0], 3, targets.shape[1]), jnp.float32)
    running_sum, unused = lax.scan(
        accumulate, zeros_init, jnp.arange(width_all // step_width, dtype=jnp.int32)
    )
    return running_sum


def on_device(
    nodal_disp,
    connect,
    brick_size,
    shear_modulus,
    bulk_modulus,
    cohesion,
    friction,
    active,
    patch_brick,
    patch_face,
    coords,
    radius,
    stiffness,
):
    segment_index = lax.axis_index("segment")
    batches = nodal_disp.shape[0]
    local_nodes = coords.shape[1]

    def fem_side(unused):
        stress, centre = brick_stress(
            nodal_disp, connect, brick_size, shear_modulus, bulk_modulus, cohesion, friction, active
        )
        traction, fem_disp = interface(stress, centre, patch_brick, patch_face)
        return jnp.stack([traction, fem_disp])

    def fem_skip(unused):
        return jnp.zeros((2, batches, 3, local_nodes), jnp.bfloat16)

    produced = lax.cond(segment_index == 0, fem_side, fem_skip, 0)
    received = from_behind(produced, "segment", 1)
    joined = jnp.where(segment_index == 0, produced, received)
    traction = joined[0]
    fem_wide = joined[1].astype(jnp.float32)
    trac_wide = traction.astype(jnp.float32)
    points = jnp.concatenate([coords, radius[None, :]], axis=0)
    zero_disp = jnp.zeros((batches, 3, local_nodes), jnp.float32)
    sources = lax.all_gather(points, ("blk", "rows"), axis=1, tiled=True)

    def add_whole(running_sum, piece_data):
        return lax.cond(
            segment_index == 1,
            lambda running: apply_piece(coords, sources, piece_data),
            lambda running: running,
            running_sum,
        )

    def sweep_whole(density):
        return add_whole(zero_disp, lax.all_gather(density, ("blk", "rows"), axis=2, tiled=True))

    displacement = sweep_whole(traction)
    for sweep_step in range(1, SWEEPS):
        density = (trac_wide - stiffness[None, None, :] * displacement).astype(jnp.bfloat16)
        displacement = sweep_whole(density)
    returned = from_behind(displacement, "segment", -1)
    displacement = jnp.where(segment_index == 0, returned, displacement)
    return fem_wide + RELAXATION * (displacement - fem_wide)


def solution(mesh):
    return jax.shard_map(
        on_device,
        mesh=mesh,
        in_specs=(
            P(None, None, ("blk", "rows")),
            P(None, ("blk", "rows")),
            P(("blk", "rows")),
            P(("blk", "rows")),
            P(("blk", "rows")),
            P(("blk", "rows")),
            P(("blk", "rows")),
            P(("blk", "rows")),
            P(("blk", "rows")),
            P(("blk", "rows")),
            P(None, ("blk", "rows")),
            P(("blk", "rows")),
            P(("blk", "rows")),
        ),
        out_specs=P(None, None, ("blk", "rows")),
        check_vma=False,
    )
```

profile of v0, /device:TPU:1, one launch (start us, length us, event | category | flops | bytes accessed | tf_op | source)
XLA Modules:
  0.0 1464.0 jit_solution(16121889803462859632)
XLA Ops:
  0.0 443.6 %conditional.4 = (bf16[2,8,3,256]{3,1,2,0:T(8,128)(2,1)S(1)}) conditional(s32[]{:T(128)} %convert_element_type.92, () %tuple.42, (s32[256]{0:T(256)}, s32[4096]{0:T(1024)}, f32[4096]{0:T(1024)}, f32[4096]{0:T(1024)}, f32[4096]{0:T(1024)}, /*index=5*/s32[8,4096]{1,0:T(8,128)}, f32[8,3,4096]{2,0,1:T(8,128)}, f32[4096]{0:T(1024)}, f32[4096]{0:T(1024)}, ...), branch_computations={%region_0.0_spmd, %region_1.5_spmd.clone} | conditional | flops 35742464 | bytes 37726972 | solution.py:133
  0.0 1.9 fusion.47
  2.0 6.6 copy.91
  8.6 33.6 %gather_fusion.2 = f32[4096,8,3]{1,2,0:T(4,128)} fusion(f32[8,3,4096]{0,1,2:T(4,128)} %copy.91, s32[4096]{0:T(1024)S(1)} %fusion.29), kind=kCustom, calls=%fused_computation.clone | custom fusion | bytes 802816 | tf_op jit(solution)/shard_map/cond/branch_1_fun/jit(_take)/gather | solution.py:37
  42.2 33.7 %gather_fusion.3 = f32[4096,8,3]{1,2,0:T(4,128)} fusion(f32[8,3,4096]{0,1,2:T(4,128)} %copy.91, s32[4096]{0:T(1024)S(1)} %fusion.30), kind=kCustom, calls=%fused_computation.1.clone | custom fusion | bytes 802816 | tf_op jit(solution)/shard_map/cond/branch_1_fun/jit(_take)/gather | solution.py:37
  75.9 33.4 %gather_fusion.4 = f32[4096,8,3]{1,2,0:T(4,128)} fusion(f32[8,3,4096]{0,1,2:T(4,128)} %copy.91, s32[4096]{0:T(1024)S(1)} %fusion.31), kind=kCustom, calls=%fused_computation.2.clone | custom fusion | bytes 802816 | tf_op jit(solution)/shard_map/cond/branch_1_fun/jit(_take)/gather | solution.py:37
  109.3 33.4 %gather_fusion.5 = f32[4096,8,3]{1,2,0:T(4,128)} fusion(f32[8,3,4096]{0,1,2:T(4,128)} %copy.91, s32[4096]{0:T(1024)S(1)} %fusion.32), kind=kCustom, calls=%fused_computation.3.clone | custom fusion | bytes 802816 | tf_op jit(solution)/shard_map/cond/branch_1_fun/jit(_take)/gather | solution.py:37
  142.7 33.6 %gather_fusion.6 = f32[4096,8,3]{1,2,0:T(4,128)} fusion(f32[8,3,4096]{0,1,2:T(4,128)} %copy.91, s32[4096]{0:T(1024)S(1)} %fusion.33), kind=kCustom, calls=%fused_computation.4.clone | custom fusion | bytes 802816 | tf_op jit(solution)/shard_map/cond/branch_1_fun/jit(_take)/gather | solution.py:37
  176.4 33.7 %gather_fusion.7 = f32[4096,8,3]{1,2,0:T(4,128)} fusion(f32[8,3,4096]{0,1,2:T(4,128)} %copy.91, s32[4096]{0:T(1024)S(1)} %fusion.34), kind=kCustom, calls=%fused_computation.5.clone | custom fusion | bytes 802816 | tf_op jit(solution)/shard_map/cond/branch_1_fun/jit(_take)/gather | solution.py:37
  210.1 33.7 %gather_fusion.8 = f32[4096,8,3]{1,2,0:T(4,128)} fusion(f32[8,3,4096]{0,1,2:T(4,128)} %copy.91, s32[4096]{0:T(1024)S(1)} %fusion.35), kind=kCustom, calls=%fused_computation.6.clone | custom fusion | bytes 802816 | tf_op jit(solution)/shard_map/cond/branch_1_fun/jit(_take)/gather | solution.py:37
  243.7 33.7 %gather_fusion.9 = f32[4096,8,3]{1,2,0:T(4,128)} fusion(f32[8,3,4096]{0,1,2:T(4,128)} %copy.91, s32[4096]{0:T(1024)S(1)} %fusion.36), kind=kCustom, calls=%fused_computation.7.clone | custom fusion | bytes 802816 | tf_op jit(solution)/shard_map/cond/branch_1_fun/jit(_take)/gather | solution.py:37
  277.5 75.7 %add_multiply_fusion = (bf16[8,3,4096]{0,1,2:T(4,128)(2,1)}, f32[8,3,4096]{0,1,2:T(4,128)}, f32[8,3,4096]{0,1,2:T(4,128)}, f32[8,3,4096]{0,1,2:T(4,128)}, f32[8,...) fusion(f32[4096,8,3]{1,2,0:T(4,128)} %gather_fusion.3, ...), kind=kLoop, calls=%fused_computation.75 | loop fusion | flops 1671168 | bytes 6520832 | tf_op jit(solution)/shard_map/cond/branch_1_fun/div | solution.py:41
  353.2 6.4 copy.72
  359.6 6.4 copy.73
  365.9 6.4 copy.74
  372.3 6.4 copy.75
  378.7 6.4 copy.76
  385.1 6.4 copy.77
  391.4 6.4 copy.78
  397.8 6.4 copy.79
  404.2 0.1 fusion.40
  404.4 1.4 add_multiply_fusion.1
  406.0 1.6 multiply_reduce_fusion.3
  407.7 2.7 multiply_add_fusion.3
  410.4 17.7 %copy.88 = f32[8,3,3,4096]{0,2,3,1:T(4,128)} copy(f32[8,3,3,4096]{3,0,2,1:T(8,128)} %multiply_add_fusion.3) | data formatting | bytes 2359296 | tf_op jit(solution)/shard_map/cond/branch_1_fun/add | solution.py:52
  428.2 9.9 gather_fusion
  438.1 0.1 fusion.27
  438.3 1.6 fusion.24
  439.9 0.1 copy.90
  440.1 3.2 gather_fusion.1
  443.3 0.1 copy.89
  443.6 1.3 collective-permute-start
  445.0 99.1 %all_gather.13 = f32[4,16384]{1,0:T(4,128)S(1)} all-gather(f32[4,256]{1,0:T(4,128)S(1)} %pad_maximum_fusion.1), channel_id=1, replica_groups=mesh['segment'=2,'blk'=8,'rows'=8] {'blk','rows'}, dimensions={1}, use_global_device_ids=true | all-gather | bytes 266240 | tf_op jit(solution)/shard_map/all_gather | solution.py:141
  544.0 90.6 %all-gather = bf16[1,8,3,16384]{3,1,2,0:T(8,128)(2,1)S(1)} all-gather(bf16[1,8,3,256]{3,1,2,0:T(8,128)(2,1)S(1)} %slice.132), channel_id=2, replica_groups=mesh['segment'=2,'blk'=8,'rows'=8] {'blk','rows'}, dimensions={3}, use_global_device_ids=true | all-gather | bytes 798720 | tf_op jit(solution)/shard_map/all_gather | solution.py:152
  634.6 0.6 conditional.5
  634.7 0.6 broadcast.413
  635.3 0.1 copy-done.7
  635.3 0.7 fusion.44
  636.1 91.9 %all_gather.14 = bf16[8,3,16384]{2,0,1:T(8,128)(2,1)S(1)} all-gather(bf16[8,3,256]{2,0,1:T(8,128)(2,1)S(1)} %fusion.44), channel_id=1, replica_groups=mesh['segment'=2,'blk'=8,'rows'=8] {'blk','rows'}, dimensions={2}, use_global_device_ids=true | all-gather | bytes 798720 | tf_op jit(solution)/shard_map/all_gather | solution.py:152
  728.0 0.6 conditional.6
  728.0 0.6 broadcast.418
  728.6 0.7 fusion.45
  729.3 90.6 %all_gather.15 = bf16[8,3,16384]{2,0,1:T(8,128)(2,1)S(1)} all-gather(bf16[8,3,256]{2,0,1:T(8,128)(2,1)S(1)} %fusion.45), channel_id=1, replica_groups=mesh['segment'=2,'blk'=8,'rows'=8] {'blk','rows'}, dimensions={2}, use_global_device_ids=true | all-gather | bytes 798720 | tf_op jit(solution)/shard_map/all_gather | solution.py:152
  819.9 0.6 conditional.7
  819.9 0.6 broadcast.423
  820.5 1.3 collective-permute-start.1
  821.8 641.6 %collective-permute-done.1 = f32[8,3,256]{2,0,1:T(8,128)S(1)} collective-permute-done((f32[8,3,256]{2,0,1:T(8,128)}, f32[8,3,256]{2,0,1:T(8,128)S(1)}, u32[]{:S(2)}, u32[]{:S(2)}) %collective-permute-start.1) | collective-permute-done | bytes 24608 | tf_op jit(solution)/shard_map/ppermute | solution.py:20
  1463.4 0.6 convert_add_fusion
  (51 shorter events, 0.4 us)
Async XLA Ops:
  0.0 444.9 %copy-start = (f32[3,256]{1,0:T(4,128)S(1)}, f32[3,256]{1,0:T(4,128)}, u32[]{:S(2)}) copy-start(f32[3,256]{1,0:T(4,128)} %param.40) | copy-start | bytes 9220
  0.0 444.9 %copy-start.10 = (f32[256]{0:T(256)S(1)}, f32[256]{0:T(256)}, u32[]{:S(2)}) copy-start(f32[256]{0:T(256)} %param.41) | copy-start | bytes 3076
  397.8 6.4 copy-start.11
  397.8 6.6 copy-start.5
  397.8 6.6 copy-start.6
  405.9 1.7 copy-start.4
  405.9 1.7 copy-start.1
  405.9 1.7 copy-start.2
  405.9 1.7 copy-start.3
  410.4 17.7 %copy-start.8 = (s32[256]{0:T(256)S(1)}, s32[256]{0:T(256)}, u32[]{:S(2)}) copy-start(s32[256]{0:T(256)} %get-tuple-element.196) | copy-start | bytes 3076 | tf_op jit(solution)/shard_map/cond
  410.4 17.7 %copy-start.9 = (s32[256]{0:T(256)S(1)}, s32[256]{0:T(256)}, u32[]{:S(2)}) copy-start(s32[256]{0:T(256)} %get-tuple-element.205) | copy-start | bytes 3076 | tf_op jit(solution)/shard_map/cond
  443.6 100.4 %collective-permute-start = (bf16[2,8,3,256]{3,1,2,0:T(8,128)(2,1)S(1)}, bf16[2,8,3,256]{3,1,2,0:T(8,128)(2,1)S(1)}, u32[]{:S(2)}, u32[]{:S(2)}) collective-permute-start(bf16[2,8,3,256]{3,1,2,0:T(8,128)(2,1)S(1)} %get-tuple-element.671), channel_id=1, source_target_pairs={{0,64},{1,65},{2,66},{3,67},{4,68},{5,69},{6,70},{7,71},{8,72},{9,... | collective-permute-start | bytes 73736 | tf_op jit(solution)/shard_map/ppermute | solution.py:20
  634.6 0.7 copy-start.7
  820.5 642.9 %collective-permute-start.1 = (f32[8,3,256]{2,0,1:T(8,128)}, f32[8,3,256]{2,0,1:T(8,128)S(1)}, u32[]{:S(2)}, u32[]{:S(2)}) collective-permute-start(f32[8,3,256]{2,0,1:T(8,128)} %get-tuple-element.674), channel_id=1, source_target_pairs={{64,0},{65,1},{66,2},{67,3},{68,4},{69,5},{70,6},{71,7},{72,8},{73... | collective-permute-start | bytes 73736 | tf_op jit(solution)/shard_map/ppermute | solution.py:20
where the time goes:
time: 1480 us; the launch traced here: 1460 us
  waiting for transfers between devices  642 us (43%)
  blocking collectives  372 us (25%)
  local copies, waits for them, and re-layouts  361 us (24%)
  other arithmetic  85.8 us (6%)
    ppermute x2, waiting for transfers between devices, from_behind(): return lax.ppermute(x, axis, pairs)  642 us
    all_gather x3, blocking collectives, sweep_whole(): lax.all_gather(density, ('blk', 'rows'), axis=2, tiled=True)  273 us
    gather x8, local copies, waits for them, and re-layouts, brick_stress(): corner_disp = jnp.take(nodal_disp, connect[corner], axis=2)  269 us
    all_gather x1, blocking collectives, on_device(): sources = lax.all_gather(points, ('blk', 'rows'), axis=1, tiled=True)  99.1 us
    div x1, other arithmetic, brick_stress(): centre = centre / 8.0  75.7 us
    select_n x8, local copies, waits for them, and re-layouts, brick_stress(): corner_disp = jnp.take(nodal_disp, connect[corner], axis=2)  51 us
  transfers between devices with their start and end apart: 2, of which 1 were waited for; matrix products, arithmetic and copies ran while one was open for 0% of the time, Pallas kernels for 0%

commit v1 on v0

v1 whole, which is shorter than its diff:
```python
import math

import jax
import jax.numpy as jnp
from jax import lax
from jax.experimental import pallas as pl
from jax.experimental.pallas import tpu as pltpu
from jax.sharding import PartitionSpec as P

SWEEPS = 3

KELVIN_A = 1.0 / (1024.0 * math.pi)
KELVIN_B = KELVIN_A / 3.0
SMOOTH = 0.1
RELAXATION = 0.5

F32 = jnp.float32
BF16 = jnp.bfloat16
MESH = pl.DeviceIdType.MESH
OWN = 128


def hops(step):
    return min(step % 4, 4 - step % 4)


SOURCE_STEPS = sorted(
    ((dz, dy) for dz in range(4) for dy in range(4)),
    key=lambda step: (hops(step[0]) + hops(step[1]), step),
)
TARGET_STEPS = [(2, 0), (2, 1), (1, 0), (1, 1), (3, 0), (3, 1), (0, 1), (0, 0)]
SLOTS = len(SOURCE_STEPS)
BLOCKS = len(TARGET_STEPS)
SOURCES = SLOTS * OWN
COMPONENTS = 6


def lane_gather(values, index):
    numbers = lax.GatherDimensionNumbers(
        offset_dims=(),
        collapsed_slice_dims=(1,),
        start_index_map=(1,),
        operand_batching_dims=(0,),
        start_indices_batching_dims=(0,),
    )
    return lax.gather(
        values,
        index[:, :, None],
        numbers,
        (1, 1),
        mode=lax.GatherScatterMode.PROMISE_IN_BOUNDS,
    )


def brick_side(refs, half, trac_ref, fem_ref):
    nodal, connect, size, shear, bulk, cohesion, friction, active, brick, face = refs
    node_brick = brick[pl.ds(half, 1), :]
    node_face = face[pl.ds(half, 1), :]
    high = jnp.broadcast_to(node_brick // 128, (8, OWN))
    low = jnp.broadcast_to(node_brick % 128, (8, OWN))

    def pick_corner(tile, corners):
        part = connect[:, pl.ds(pl.multiple_of(tile * 128, 128), 128)]
        return jnp.where(high == tile, lane_gather(part, low), corners)

    corners = lax.fori_loop(0, 32, pick_corner, jnp.zeros((8, OWN), jnp.int32), unroll=8)
    row = lax.broadcasted_iota(jnp.int32, (8, OWN), 0)

    def pick(values):
        total = jnp.zeros((8, OWN), F32)
        for group in range(4):
            part = lane_gather(values[8 * group : 8 * group + 8], low)
            total = total + jnp.where(high == row + 8 * group, part, 0.0)
        return jnp.sum(total, axis=0, keepdims=True)

    size_at = pick(size[...])
    shear_at = pick(shear[...])
    bulk_at = pick(bulk[...])
    cohesion_at = pick(cohesion[...])
    friction_at = pick(friction[...])
    active_at = pick(jnp.where(active[...] == 1, 1.0, 0.0))

    corner_high = [jnp.broadcast_to(corners[c : c + 1] // 128, (8, OWN)) for c in range(8)]
    corner_low = [jnp.broadcast_to(corners[c : c + 1] % 128, (8, OWN)) for c in range(8)]

    def pick_nodes(tile, picked):
        columns = pl.ds(pl.multiple_of(tile * 128, 128), 128)
        parts = [nodal[i, :, columns] for i in range(3)]
        out = []
        for c in range(8):
            here = corner_high[c] == tile
            for i in range(3):
                out.append(
                    jnp.where(here, lane_gather(parts[i], corner_low[c]), picked[3 * c + i])
                )
        return tuple(out)

    zero = jnp.zeros((8, OWN), F32)
    picked = lax.fori_loop(0, 32, pick_nodes, (zero,) * 24)

    gradient = [[zero] * 3 for _ in range(3)]
    centre = [zero] * 3
    for c in range(8):
        for i in range(3):
            value = picked[3 * c + i]
            centre[i] = centre[i] + value
            for j in range(3):
                if (c >> j) & 1:
                    gradient[i][j] = gradient[i][j] + value
                else:
                    gradient[i][j] = gradient[i][j] - value
    divisor = 4.0 * size_at
    gradient = [[g / divisor for g in line] for line in gradient]
    centre = [value / 8.0 for value in centre]
    strain = [[0.5 * (gradient[i][j] + gradient[j][i]) for j in range(3)] for i in range(3)]
    volume = strain[0][0] + strain[1][1] + strain[2][2]
    pressure = bulk_at * volume
    third = volume / 3.0
    deviator = [
        [2.0 * shear_at * (strain[i][j] - (third if i == j else 0.0)) for j in range(3)]
        for i in range(3)
    ]
    second = zero
    for i in range(3):
        for j in range(3):
            second = second + deviator[i][j] * deviator[i][j]
    second = 0.5 * second
    scaling = jnp.maximum(cohesion_at - friction_at * pressure, SMOOTH) / jnp.sqrt(
        second + SMOOTH * SMOOTH
    )
    scaling = jnp.where(active_at == 1.0, scaling, 1.0)
    axis_of = node_face // 2
    sign = (1 - 2 * (node_face % 2)).astype(F32)
    for i in range(3):
        line = [scaling * deviator[i][k] + (pressure if i == k else 0.0) for k in range(3)]
        chosen = jnp.where(axis_of == 0, line[0], jnp.where(axis_of == 1, line[1], line[2]))
        trac_ref[i] = (chosen * sign).astype(BF16).astype(F32)
        fem_ref[i] = centre[i].astype(BF16).astype(F32)


def kelvin_components(source, target):
    sx, sy, sz, spread, spread_more = source
    dx, dy, dz = target[0] - sx, target[1] - sy, target[2] - sz
    xx, yy, zz = dx * dx, dy * dy, dz * dz
    squared = ((xx + yy) + zz) + spread
    common = squared + (squared + spread_more)
    inverse = lax.rsqrt(squared)
    weight = (inverse * inverse) * (inverse * KELVIN_B)
    wx, wy = weight * dx, weight * dy
    return (
        weight * (xx + common),
        wx * dy,
        wx * dz,
        weight * (yy + common),
        wy * dz,
        weight * (zz + common),
    )


def kernel(
    nodal_hbm,
    connect_hbm,
    size_ref,
    shear_ref,
    bulk_ref,
    cohesion_ref,
    friction_ref,
    active_ref,
    brick_ref,
    face_ref,
    coords_ref,
    radius_ref,
    stiffness_ref,
    out_ref,
    nodal,
    connect,
    own_place,
    source_place,
    target_place,
    source_wide,
    tile,
    density,
    partial,
    arrived,
    trac,
    fem,
    result,
    local_sem,
    place_send,
    place_recv,
    target_send,
    target_recv,
    density_send,
    density_recv,
    partial_send,
    partial_recv,
    result_send,
    result_recv,
):
    half = lax.axis_index("segment")
    blk = lax.axis_index("blk")
    rows = lax.axis_index("rows")
    z, y = blk // 2, (blk % 2) * 2 + half
    x, core = rows // 2, rows % 2

    def source_peer(slot):
        dz, dy = SOURCE_STEPS[slot]
        pz, py = (z + dz) % 4, (y + dy) % 4
        return (py % 2, pz * 2 + py // 2, rows)

    def target_peer(block, sign=1):
        dx, dc = TARGET_STEPS[block]
        px, pc = (x + 4 + sign * dx) % 4, (core + dc) % 2
        return (half, blk, px * 2 + pc)

    load_nodal = pltpu.make_async_copy(nodal_hbm, nodal, local_sem.at[0])
    load_connect = pltpu.make_async_copy(connect_hbm, connect, local_sem.at[1])
    load_connect.start()
    load_nodal.start()

    barrier = pltpu.get_barrier_semaphore()
    for slot in range(1, SLOTS):
        pl.semaphore_signal(barrier, inc=1, device_id=source_peer(slot), device_id_type=MESH)
    for block in range(BLOCKS - 1):
        pl.semaphore_signal(barrier, inc=1, device_id=target_peer(block), device_id_type=MESH)

    own = pl.ds(pl.multiple_of(half * OWN, OWN), OWN)
    radius = radius_ref[pl.ds(half, 1), :]
    own_place[0:3, :] = coords_ref[:, own]
    own_place[3:4, :] = radius * radius
    own_place[4:8, :] = jnp.zeros((4, OWN), F32)
    source_place[0] = own_place[...]
    target_place[BLOCKS - 1] = own_place[...]

    pl.semaphore_wait(barrier, SLOTS - 1 + BLOCKS - 1)

    def place_copy(slot):
        return pltpu.make_async_remote_copy(
            src_ref=own_place,
            dst_ref=source_place.at[slot],
            send_sem=place_send.at[slot],
            recv_sem=place_recv.at[slot],
            device_id=source_peer(slot),
            device_id_type=MESH,
        )

    def target_copy(block):
        return pltpu.make_async_remote_copy(
            src_ref=own_place,
            dst_ref=target_place.at[block],
            send_sem=target_send.at[block],
            recv_sem=target_recv.at[block],
            device_id=target_peer(block, -1),
            device_id_type=MESH,
        )

    def density_copy(sweep, slot):
        return pltpu.make_async_remote_copy(
            src_ref=density.at[sweep, 0],
            dst_ref=density.at[sweep, slot],
            send_sem=density_send.at[sweep, slot],
            recv_sem=density_recv.at[sweep, slot],
            device_id=source_peer(slot),
            device_id_type=MESH,
        )

    def partial_copy(sweep, block):
        return pltpu.make_async_remote_copy(
            src_ref=partial.at[sweep, block],
            dst_ref=arrived.at[sweep, block],
            send_sem=partial_send.at[sweep, block],
            recv_sem=partial_recv.at[sweep, block],
            device_id=target_peer(block),
            device_id_type=MESH,
        )

    for slot in range(1, SLOTS):
        place_copy(slot).start()
    for block in range(BLOCKS - 1):
        target_copy(block).start()

    def publish(sweep, values):
        density[sweep, 0] = jnp.concatenate(
            [values[0], values[1], values[2], values[0]], axis=0
        ).astype(BF16)
        for slot in range(1, SLOTS):
            density_copy(sweep, slot).start()

    load_connect.wait()
    load_nodal.wait()
    brick_side(
        (
            nodal,
            connect,
            size_ref,
            shear_ref,
            bulk_ref,
            cohesion_ref,
            friction_ref,
            active_ref,
            brick_ref,
            face_ref,
        ),
        half,
        trac,
        fem,
    )
    publish(0, [trac[i] for i in range(3)])

    for slot in range(1, SLOTS):
        place_copy(slot).wait()
    for block in range(BLOCKS - 1):
        target_copy(block).wait()

    @pl.loop(0, SLOTS)
    def _(slot):
        columns = jnp.transpose(source_place[slot])
        place = pl.ds(pl.multiple_of(slot * OWN, OWN), OWN)
        for i in range(4):
            wide = jnp.broadcast_to(columns[:, i : i + 1], (OWN, 128))
            source_wide[i, place, :] = wide
            if i == 3:
                source_wide[4, place, :] = 1.5 * wide

    @pl.loop(0, BLOCKS)
    def _(block):
        target = [
            jnp.broadcast_to(target_place[block, i : i + 1, :], (16, OWN)) for i in range(3)
        ]

        @pl.loop(0, SOURCES // 128)
        def _(chunk):
            for step in range(8):
                place = pl.ds(pl.multiple_of(chunk * 128 + step * 16, 16), 16)
                source = [source_wide[i, place, :] for i in range(5)]
                values = kelvin_components(source, target)
                for k in range(COMPONENTS):
                    tile[k, block, place, :] = values[k].astype(BF16)

    @pl.loop(0, SWEEPS)
    def _(sweep):
        for slot in range(1, SLOTS):
            density_copy(sweep, slot).wait_recv()
        xy = jnp.concatenate([density[sweep, slot, 0:16, :] for slot in range(SLOTS)], axis=1)
        zx = jnp.concatenate([density[sweep, slot, 16:32, :] for slot in range(SLOTS)], axis=1)
        xyz = jnp.concatenate([xy, zx], axis=0)
        for pair in range(0, BLOCKS, 2):

            def product(left, k):
                right = jnp.concatenate([tile[k, pair], tile[k, pair + 1]], axis=1)
                return jnp.dot(left, right, preferred_element_type=F32)

            p_xx = product(xy, 0)
            p_xy = product(xy, 1)
            p_xz = product(zx, 2)
            p_yy = product(xy, 3)
            p_yz = product(xyz, 4)
            p_zz = product(zx, 5)
            g_x = p_xx[0:8] + p_xy[8:16] + p_xz[0:8]
            g_y = p_xy[0:8] + p_yy[8:16] + p_yz[16:24]
            g_z = p_xz[8:16] + p_yz[8:16] + p_zz[0:8]
            for block in (pair, pair + 1):
                lanes = slice((block - pair) * OWN, (block - pair + 1) * OWN)
                partial[sweep, block, 0] = g_x[:, lanes]
                partial[sweep, block, 1] = g_y[:, lanes]
                partial[sweep, block, 2] = g_z[:, lanes]
                if block < BLOCKS - 1:
                    partial_copy(sweep, block).start()
        total = [partial[sweep, BLOCKS - 1, i] for i in range(3)]
        for block in range(BLOCKS - 1):
            partial_copy(sweep, block).wait_recv()
            for i in range(3):
                total[i] = total[i] + arrived[sweep, block, i]

        @pl.when(sweep < SWEEPS - 1)
        def _():
            stiffness = stiffness_ref[pl.ds(half, 1), :]
            publish(sweep + 1, [trac[i] - stiffness * total[i] for i in range(3)])

        @pl.when(sweep == SWEEPS - 1)
        def _():
            for i in range(3):
                fem_wide = fem[i]
                result[half, i] = fem_wide + RELAXATION * (total[i] - fem_wide)

    exchange = pltpu.make_async_remote_copy(
        src_ref=result.at[half],
        dst_ref=result.at[half],
        send_sem=result_send,
        recv_sem=result_recv,
        device_id=((half + 1) % 2, blk, rows),
        device_id_type=MESH,
    )
    exchange.start()

    @pl.loop(0, SWEEPS)
    def _(sweep):
        for slot in range(1, SLOTS):
            density_copy(sweep, slot).wait_send()
        for block in range(BLOCKS - 1):
            partial_copy(sweep, block).wait_send()

    exchange.wait()
    for i in range(3):
        out_ref[i] = jnp.concatenate([result[0, i], result[1, i]], axis=1)


def on_device(
    nodal_disp,
    connect,
    brick_size,
    shear_modulus,
    bulk_modulus,
    cohesion,
    friction,
    active,
    patch_brick,
    patch_face,
    coords,
    radius,
    stiffness,
):
    batches = nodal_disp.shape[0]
    local_nodes = coords.shape[1]
    anywhere = pl.BlockSpec(memory_space=pl.ANY)
    vmem = pl.BlockSpec(memory_space=pltpu.VMEM)
    dma = pltpu.SemaphoreType.DMA
    by_brick = [
        values.reshape(-1, 128)
        for values in (brick_size, shear_modulus, bulk_modulus, cohesion, friction, active)
    ]
    by_node = [values.reshape(-1, OWN) for values in (patch_brick, patch_face)]
    relaxed = pl.pallas_call(
        kernel,
        out_shape=jax.ShapeDtypeStruct((3, batches, local_nodes), F32),
        in_specs=[anywhere] * 2 + [vmem] * 11,
        out_specs=vmem,
        scratch_shapes=[
            pltpu.VMEM((3, batches, nodal_disp.shape[2]), F32),
            pltpu.VMEM(connect.shape, jnp.int32),
            pltpu.VMEM((8, OWN), F32),
            pltpu.VMEM((SLOTS, 8, OWN), F32),
            pltpu.VMEM((BLOCKS, 8, OWN), F32),
            pltpu.VMEM((5, SOURCES, 128), F32),
            pltpu.VMEM((COMPONENTS, BLOCKS, SOURCES, 128), BF16),
            pltpu.VMEM((SWEEPS, SLOTS, 32, OWN), BF16),
            pltpu.VMEM((SWEEPS, BLOCKS, 3, 8, OWN), F32),
            pltpu.VMEM((SWEEPS, BLOCKS, 3, 8, OWN), F32),
            pltpu.VMEM((3, 8, OWN), F32),
            pltpu.VMEM((3, 8, OWN), F32),
            pltpu.VMEM((2, 3, 8, OWN), F32),
            dma((2,)),
            dma((SLOTS,)),
            dma((SLOTS,)),
            dma((BLOCKS,)),
            dma((BLOCKS,)),
            dma((SWEEPS, SLOTS)),
            dma((SWEEPS, SLOTS)),
            dma((SWEEPS, BLOCKS)),
            dma((SWEEPS, BLOCKS)),
            dma,
            dma,
        ],
        compiler_params=pltpu.CompilerParams(
            collective_id=0, has_side_effects=True, vmem_limit_bytes=50 * 2**20
        ),
    )(
        nodal_disp.transpose(1, 0, 2),
        connect,
        *by_brick,
        *by_node,
        coords,
        radius.reshape(-1, OWN),
        stiffness.reshape(-1, OWN),
    )
    return relaxed.transpose(1, 0, 2)


def solution(mesh):
    split = ("blk", "rows")
    return jax.shard_map(
        on_device,
        mesh=mesh,
        in_specs=(
            P(None, None, split),
            P(None, split),
            P(split),
            P(split),
            P(split),
            P(split),
            P(split),
            P(split),
            P(split),
            P(split),
            P(None, split),
            P(split),
            P(split),
        ),
        out_specs=P(None, None, split),
        check_vma=False,
    )
```

time: 1480 us -> 67.4 us (0.05); the launches traced: 1460 us -> 66.7 us
  waiting for transfers between devices: 642 us -> 0 us
  blocking collectives: 372 us -> 0 us
  local copies, waits for them, and re-layouts: 361 us -> 9.53 us
  other arithmetic: 85.8 us -> 0 us
  Pallas kernels: 0 us -> 57.2 us
    ppermute x2 -> x0, waiting for transfers between devices: 642 us -> none  [from_behind(): return lax.ppermute(x, axis, pairs)]
    all_gather x4 -> x0, blocking collectives: 372 us -> none  [the longest x3 273 us: sweep_whole(): lax.all_gather(density, ('blk', 'rows'), axis=2, tiled=True)]
    gather x11 -> x0, local copies, waits for them, and re-layouts: 282 us -> none  [the longest x8 269 us: brick_stress(): corner_disp = jnp.take(nodal_disp, connect[corner], axis=2)]
    div x1 -> x0, other arithmetic: 75.7 us -> none  [brick_stress(): centre = centre / 8.0]
    pallas_call x0 -> x1, Pallas kernels: none -> 57.2 us  [on_device(): pl.pallas_call(kernel, out_shape=jax.ShapeDtypeStruct((3, batches, local_...]
    select_n x8 -> x0, local copies, waits for them, and re-layouts: 51 us -> none  [brick_stress(): corner_disp = jnp.take(nodal_disp, connect[corner], axis=2)]
    add x1 -> x0, local copies, waits for them, and re-layouts: 17.7 us -> none  [brick_stress(): scaling[:, None, None, :] * deviator + pressure[:, None, None, :] * identity]
  transfers between devices with their start and end apart: 2 -> 0, of which waited for: 1 -> 0; matrix products, arithmetic and copies ran while one was open for 0% -> 0% of each run, Pallas kernels for 0% -> 0%
where the time goes in v1:
time: 67.4 us; the launch traced here: 66.7 us
  Pallas kernels  57.2 us (85%)
  local copies, waits for them, and re-layouts  9.53 us (14%)
    pallas_call x1, Pallas kernels, on_device(): pl.pallas_call(kernel, out_shape=jax.ShapeDtypeStruct((3, batches, local_...  57.2 us
    unnamed x27, local copies, waits for them, and re-layouts  9.53 us

profile of v1, /device:TPU:1, one launch (start us, length us, event | category | flops | bytes accessed | tf_op | source)
XLA Modules:
  0.0 66.7 jit_solution(8489064957759000073)
XLA Ops:
  0.0 0.0 copy-start.2
  0.0 0.0 copy-start.8
  0.0 0.7 %copy-done.2 = f32[4096]{0:T(1024)S(1)} copy-done((f32[4096]{0:T(1024)S(1)}, f32[4096]{0:T(1024)}, u32[]{:S(2)}) %copy-start.2) | copy-done | bytes 16408
  0.7 0.0 copy-done.8
  0.7 0.0 copy-start
  0.7 1.0 %copy-done = f32[8,3,4096]{2,0,1:T(8,128)S(1)} copy-done((f32[8,3,4096]{2,0,1:T(8,128)S(1)}, f32[8,3,4096]{2,0,1:T(8,128)}, u32[]{:S(2)}) %copy-start) | copy-done | bytes 393240
  1.7 0.0 copy-start.1
  1.7 0.9 %copy-done.1 = s32[8,4096]{1,0:T(8,128)S(1)} copy-done((s32[8,4096]{1,0:T(8,128)S(1)}, s32[8,4096]{1,0:T(8,128)}, u32[]{:S(2)}) %copy-start.1) | copy-done | bytes 131096
  2.6 0.0 copy-start.3
  2.6 0.7 %copy-done.3 = f32[4096]{0:T(1024)S(1)} copy-done((f32[4096]{0:T(1024)S(1)}, f32[4096]{0:T(1024)}, u32[]{:S(2)}) %copy-start.3) | copy-done | bytes 16408
  3.3 0.0 copy-start.4
  3.3 0.7 %copy-done.4 = f32[4096]{0:T(1024)S(1)} copy-done((f32[4096]{0:T(1024)S(1)}, f32[4096]{0:T(1024)}, u32[]{:S(2)}) %copy-start.4) | copy-done | bytes 16408
  4.1 0.0 copy-start.5
  4.1 0.7 %copy-done.5 = f32[4096]{0:T(1024)S(1)} copy-done((f32[4096]{0:T(1024)S(1)}, f32[4096]{0:T(1024)}, u32[]{:S(2)}) %copy-start.5) | copy-done | bytes 16408
  4.8 0.0 copy-start.6
  4.8 0.7 %copy-done.6 = f32[4096]{0:T(1024)S(1)} copy-done((f32[4096]{0:T(1024)S(1)}, f32[4096]{0:T(1024)}, u32[]{:S(2)}) %copy-start.6) | copy-done | bytes 16408
  5.5 0.0 copy-start.7
  5.5 0.7 %copy-done.7 = s32[4096]{0:T(1024)S(1)} copy-done((s32[4096]{0:T(1024)S(1)}, s32[4096]{0:T(1024)}, u32[]{:S(2)}) %copy-start.7) | copy-done | bytes 16408
  6.2 0.0 copy-start.9
  6.2 0.7 %copy-done.9 = s32[256]{0:T(256)S(1)} copy-done((s32[256]{0:T(256)S(1)}, s32[256]{0:T(256)}, u32[]{:S(2)}) %copy-start.9) | copy-done | bytes 1048
  6.9 0.0 copy-start.10
  6.9 0.7 %copy-done.10 = s32[256]{0:T(256)S(1)} copy-done((s32[256]{0:T(256)S(1)}, s32[256]{0:T(256)}, u32[]{:S(2)}) %copy-start.10) | copy-done | bytes 1048
  7.6 0.0 copy-start.11
  7.6 0.7 %copy-done.11 = f32[256]{0:T(256)S(1)} copy-done((f32[256]{0:T(256)S(1)}, f32[256]{0:T(256)}, u32[]{:S(2)}) %copy-start.11) | copy-done | bytes 1048
  8.3 0.0 copy-start.12
  8.3 0.7 %copy-done.12 = f32[256]{0:T(256)S(1)} copy-done((f32[256]{0:T(256)S(1)}, f32[256]{0:T(256)}, u32[]{:S(2)}) %copy-start.12) | copy-done | bytes 1048
  8.9 57.2 %shard_map.127 = f32[3,8,256]{2,1,0:T(8,128)S(1)} custom-call(f32[3,8,4096]{2,1,0:T(8,128)S(1)} %bitcast.12, s32[8,4096]{1,0:T(8,128)S(1)} %copy-done.1, f32[32,128]{1,0:T(8,128)S(1)} %bitcast.14, f32[32,128]{1,0:T(8,128)S(1)} %bitcast.15, f32[32,128]{1,0:T(8,128)S(1)} %bitcast.16, f32[32,128]{1,0:T(8,128)S(1)} %bitcast.17, f32[32,128]{1,0:T(8,128)S(1)} %bitcast.18, ...), custom_call_target="tpu_custom_call" | custom-call | tf_op jit(solution)/shard_map/pallas_call | solution.py:433
  66.1 0.6 copy.15
Async XLA Ops:
  0.0 0.7 %copy-start.2 = (f32[4096]{0:T(1024)S(1)}, f32[4096]{0:T(1024)}, u32[]{:S(2)}) copy-start(f32[4096]{0:T(1024)} %param.15) | copy-start | bytes 49156
  0.0 0.7 %copy-start.8 = (f32[3,256]{1,0:T(4,128)S(1)}, f32[3,256]{1,0:T(4,128)}, u32[]{:S(2)}) copy-start(f32[3,256]{1,0:T(4,128)} %coords_ref.1) | copy-start | bytes 9220
  0.7 1.0 %copy-start = (f32[8,3,4096]{2,0,1:T(8,128)S(1)}, f32[8,3,4096]{2,0,1:T(8,128)}, u32[]{:S(2)}) copy-start(f32[8,3,4096]{2,0,1:T(8,128)} %param.13) | copy-start | bytes 1179652
  1.7 0.9 %copy-start.1 = (s32[8,4096]{1,0:T(8,128)S(1)}, s32[8,4096]{1,0:T(8,128)}, u32[]{:S(2)}) copy-start(s32[8,4096]{1,0:T(8,128)} %connect_hbm.1) | copy-start | bytes 393220
  2.6 0.7 %copy-start.3 = (f32[4096]{0:T(1024)S(1)}, f32[4096]{0:T(1024)}, u32[]{:S(2)}) copy-start(f32[4096]{0:T(1024)} %param.16) | copy-start | bytes 49156
  3.3 0.7 %copy-start.4 = (f32[4096]{0:T(1024)S(1)}, f32[4096]{0:T(1024)}, u32[]{:S(2)}) copy-start(f32[4096]{0:T(1024)} %param.17) | copy-start | bytes 49156
  4.1 0.7 %copy-start.5 = (f32[4096]{0:T(1024)S(1)}, f32[4096]{0:T(1024)}, u32[]{:S(2)}) copy-start(f32[4096]{0:T(1024)} %param.18) | copy-start | bytes 49156
  4.8 0.7 %copy-start.6 = (f32[4096]{0:T(1024)S(1)}, f32[4096]{0:T(1024)}, u32[]{:S(2)}) copy-start(f32[4096]{0:T(1024)} %param.19) | copy-start | bytes 49156
  5.5 0.7 %copy-start.7 = (s32[4096]{0:T(1024)S(1)}, s32[4096]{0:T(1024)}, u32[]{:S(2)}) copy-start(s32[4096]{0:T(1024)} %param.20) | copy-start | bytes 49156
  6.2 0.7 %copy-start.9 = (s32[256]{0:T(256)S(1)}, s32[256]{0:T(256)}, u32[]{:S(2)}) copy-start(s32[256]{0:T(256)} %param.21) | copy-start | bytes 3076
  6.9 0.7 %copy-start.10 = (s32[256]{0:T(256)S(1)}, s32[256]{0:T(256)}, u32[]{:S(2)}) copy-start(s32[256]{0:T(256)} %param.22) | copy-start | bytes 3076
  7.6 0.7 %copy-start.11 = (f32[256]{0:T(256)S(1)}, f32[256]{0:T(256)}, u32[]{:S(2)}) copy-start(f32[256]{0:T(256)} %param.24) | copy-start | bytes 3076
  8.3 0.7 %copy-start.12 = (f32[256]{0:T(256)S(1)}, f32[256]{0:T(256)}, u32[]{:S(2)}) copy-start(f32[256]{0:T(256)} %param.25) | copy-start | bytes 3076

commit v2 on v1

--- a/solution.py
+++ b/solution.py
@@ -32,6 +32,10 @@
 SLOTS = len(SOURCE_STEPS)
 BLOCKS = len(TARGET_STEPS)
 SOURCES = SLOTS * OWN
+PAIRS = BLOCKS // 2
+CHUNKS = SLOTS // 2
+NEAR = 2
+GROUPS = ((0, 2), (2, 6))
 COMPONENTS = 6
 
 
@@ -63,7 +67,7 @@
         part = connect[:, pl.ds(pl.multiple_of(tile * 128, 128), 128)]
         return jnp.where(high == tile, lane_gather(part, low), corners)
 
-    corners = lax.fori_loop(0, 32, pick_corner, jnp.zeros((8, OWN), jnp.int32), unroll=8)
+    corners = lax.fori_loop(0, 32, pick_corner, jnp.zeros((8, OWN), jnp.int32), unroll=16)
     row = lax.broadcasted_iota(jnp.int32, (8, OWN), 0)
 
     def pick(values):
@@ -83,20 +87,19 @@
     corner_high = [jnp.broadcast_to(corners[c : c + 1] // 128, (8, OWN)) for c in range(8)]
     corner_low = [jnp.broadcast_to(corners[c : c + 1] % 128, (8, OWN)) for c in range(8)]
 
-    def pick_nodes(tile, picked):
-        columns = pl.ds(pl.multiple_of(tile * 128, 128), 128)
-        parts = [nodal[i, :, columns] for i in range(3)]
-        out = []
-        for c in range(8):
+    zero = jnp.zeros((8, OWN), F32)
+    picked = []
+    for c in range(8):
+
+        def pick_nodes(tile, values, c=c):
+            columns = pl.ds(pl.multiple_of(tile * 128, 128), 128)
             here = corner_high[c] == tile
-            for i in range(3):
-                out.append(
-                    jnp.where(here, lane_gather(parts[i], corner_low[c]), picked[3 * c + i])
-                )
-        return tuple(out)
-
-    zero = jnp.zeros((8, OWN), F32)
-    picked = lax.fori_loop(0, 32, pick_nodes, (zero,) * 24)
+            return tuple(
+                jnp.where(here, lane_gather(nodal[i, :, columns], corner_low[c]), values[i])
+                for i in range(3)
+            )
+
+        picked.extend(lax.fori_loop(0, 32, pick_nodes, (zero,) * 3, unroll=16))
 
     gradient = [[zero] * 3 for _ in range(3)]
     centre = [zero] * 3
@@ -135,7 +138,7 @@
         line = [scaling * deviator[i][k] + (pressure if i == k else 0.0) for k in range(3)]
         chosen = jnp.where(axis_of == 0, line[0], jnp.where(axis_of == 1, line[1], line[2]))
         trac_ref[i] = (chosen * sign).astype(BF16).astype(F32)
-        fem_ref[i] = centre[i].astype(BF16).astype(F32)
+        fem_ref[0, i] = centre[i].astype(BF16).astype(F32)
 
 
 def kelvin_components(source, target):
@@ -160,6 +163,20 @@
 def kernel(
     nodal_hbm,
     connect_hbm,
+    size_hbm,
+    shear_hbm,
+    bulk_hbm,
+    cohesion_hbm,
+    friction_hbm,
+    active_hbm,
+    brick_hbm,
+    face_hbm,
+    coords_hbm,
+    radius_hbm,
+    stiffness_hbm,
+    out_ref,
+    nodal,
+    connect,
     size_ref,
     shear_ref,
     bulk_ref,
@@ -171,9 +188,6 @@
     coords_ref,
     radius_ref,
     stiffness_ref,
-    out_ref,
-    nodal,
-    connect,
     own_place,
     source_place,
     target_place,
@@ -184,7 +198,7 @@
     arrived,
     trac,
     fem,
-    result,
+    beside,
     local_sem,
     place_send,
     place_recv,
@@ -194,8 +208,10 @@
     density_recv,
     partial_send,
     partial_recv,
-    result_send,
-    result_recv,
+    beside_send,
+    beside_recv,
+    fem_send,
+    fem_recv,
 ):
     half = lax.axis_index("segment")
     blk = lax.axis_index("blk")
@@ -213,17 +229,40 @@
         px, pc = (x + 4 + sign * dx) % 4, (core + dc) % 2
         return (half, blk, px * 2 + pc)
 
-    load_nodal = pltpu.make_async_copy(nodal_hbm, nodal, local_sem.at[0])
-    load_connect = pltpu.make_async_copy(connect_hbm, connect, local_sem.at[1])
-    load_connect.start()
-    load_nodal.start()
+    def beside_peer(block):
+        _, _, peer_rows = target_peer(block)
+        return ((half + 1) % 2, blk, peer_rows)
+
+    place_loads = [(coords_hbm, coords_ref), (radius_hbm, radius_ref)]
+    brick_loads = [
+        (brick_hbm, brick_ref),
+        (connect_hbm, connect),
+        (nodal_hbm, nodal),
+        (face_hbm, face_ref),
+        (size_hbm, size_ref),
+        (shear_hbm, shear_ref),
+        (bulk_hbm, bulk_ref),
+        (cohesion_hbm, cohesion_ref),
+        (friction_hbm, friction_ref),
+        (active_hbm, active_ref),
+        (stiffness_hbm, stiffness_ref),
+    ]
+    loads = [
+        pltpu.make_async_copy(source, target, local_sem.at[i])
+        for i, (source, target) in enumerate(place_loads + brick_loads)
+    ]
+    for load in loads:
+        load.start()
 
     barrier = pltpu.get_barrier_semaphore()
     for slot in range(1, SLOTS):
         pl.semaphore_signal(barrier, inc=1, device_id=source_peer(slot), device_id_type=MESH)
     for block in range(BLOCKS - 1):
         pl.semaphore_signal(barrier, inc=1, device_id=target_peer(block), device_id_type=MESH)
-
+        pl.semaphore_signal(barrier, inc=1, device_id=beside_peer(block), device_id_type=MESH)
+
+    for load in loads[: len(place_loads)]:
+        load.wait()
     own = pl.ds(pl.multiple_of(half * OWN, OWN), OWN)
     radius = radius_ref[pl.ds(half, 1), :]
     own_place[0:3, :] = coords_ref[:, own]
@@ -232,7 +271,8 @@
     source_place[0] = own_place[...]
     target_place[BLOCKS - 1] = own_place[...]
 
-    pl.semaphore_wait(barrier, SLOTS - 1 + BLOCKS - 1)
+    for load in loads[len(place_loads) :]:
+        load.wait()
 
     def place_copy(slot):
         return pltpu.make_async_remote_copy(
@@ -274,20 +314,112 @@
             device_id_type=MESH,
         )
 
-    for slot in range(1, SLOTS):
-        place_copy(slot).start()
-    for block in range(BLOCKS - 1):
-        target_copy(block).start()
-
-    def publish(sweep, values):
+    def beside_copy(block):
+        return pltpu.make_async_remote_copy(
+            src_ref=partial.at[SWEEPS - 1, block],
+            dst_ref=beside.at[block],
+            send_sem=beside_send.at[block],
+            recv_sem=beside_recv.at[block],
+            device_id=beside_peer(block),
+            device_id_type=MESH,
+        )
+
+    def fem_copy():
+        return pltpu.make_async_remote_copy(
+            src_ref=fem.at[0],
+            dst_ref=fem.at[1],
+            send_sem=fem_send,
+            recv_sem=fem_recv,
+            device_id=beside_peer(BLOCKS - 1),
+            device_id_type=MESH,
+        )
+
+    def send_density(sweep, values):
         density[sweep, 0] = jnp.concatenate(
             [values[0], values[1], values[2], values[0]], axis=0
         ).astype(BF16)
-        for slot in range(1, SLOTS):
-            density_copy(sweep, slot).start()
-
-    load_connect.wait()
-    load_nodal.wait()
+
+        def start():
+            for slot in reversed(range(1, SLOTS)):
+                density_copy(sweep, slot).start()
+
+        return start
+
+    def widen(slot):
+        columns = jnp.transpose(source_place[slot])
+        place = pl.ds(pl.multiple_of(slot * OWN, OWN), OWN)
+        for i in range(4):
+            wide = jnp.broadcast_to(columns[:, i : i + 1], (OWN, 128))
+            source_wide[i, place, :] = wide
+            if i == 3:
+                source_wide[4, place, :] = 1.5 * wide
+
+    def tile_piece(pair, chunk):
+        for block in (2 * pair, 2 * pair + 1):
+            target = [
+                jnp.broadcast_to(target_place[block, i : i + 1, :], (16, OWN)) for i in range(3)
+            ]
+
+            @pl.loop(0, 2)
+            def _(part):
+                for step in range(8):
+                    first = chunk * 256 + part * 128 + step * 16
+                    place = pl.ds(pl.multiple_of(first, 16), 16)
+                    source = [source_wide[i, place, :] for i in range(5)]
+                    values = kelvin_components(source, target)
+                    for k in range(COMPONENTS):
+                        tile[k, block, place, :] = values[k].astype(BF16)
+
+    def product(sweep, blocks, chunk, chunks):
+        slots = range(2 * chunks)
+        xy = jnp.concatenate([density[sweep, 2 * chunk + i, 0:16, :] for i in slots], axis=1)
+        zx = jnp.concatenate([density[sweep, 2 * chunk + i, 16:32, :] for i in slots], axis=1)
+        xyz = jnp.concatenate([xy, zx], axis=0)
+        place = pl.ds(pl.multiple_of(chunk * 256, 256), chunks * 256)
+
+        def dot(left, k):
+            right = jnp.concatenate([tile[k, block, place, :] for block in blocks], axis=1)
+            return jnp.dot(left, right, preferred_element_type=F32)
+
+        p_xx = dot(xy, 0)
+        p_xy = dot(xy, 1)
+        p_xz = dot(zx, 2)
+        p_yy = dot(xy, 3)
+        p_yz = dot(xyz, 4)
+        p_zz = dot(zx, 5)
+        return (
+            p_xx[0:8] + p_xy[8:16] + p_xz[0:8],
+            p_xy[0:8] + p_yy[8:16] + p_yz[16:24],
+            p_xz[8:16] + p_yz[8:16] + p_zz[0:8],
+        )
+
+    def accumulate(sweep, blocks, sums, first):
+        for part, block in enumerate(blocks):
+            for i in range(3):
+                value = sums[i][:, part * OWN : (part + 1) * OWN]
+                if not first:
+                    value = value + partial[sweep, block, i]
+                partial[sweep, block, i] = value
+
+    def send_partial(sweep, blocks):
+        for block in blocks:
+            if block < BLOCKS - 1:
+                partial_copy(sweep, block).start()
+
+    def total_of(sweep):
+        total = [partial[sweep, BLOCKS - 1, i] for i in range(3)]
+        for block in reversed(range(BLOCKS - 1)):
+            partial_copy(sweep, block).wait_recv()
+            for i in range(3):
+                total[i] = total[i] + arrived[sweep, block, i]
+        return total
+
+    stiffness = stiffness_ref[pl.ds(half, 1), :]
+
+    def next_density(sweep):
+        total = total_of(sweep)
+        send_density(sweep + 1, [trac[i] - stiffness * total[i] for i in range(3)])()
+
     brick_side(
         (
             nodal,
@@ -305,93 +437,87 @@
         trac,
         fem,
     )
-    publish(0, [trac[i] for i in range(3)])
+    start_density = send_density(0, [trac[i] for i in range(3)])
+    widen(0)
+
+    pl.semaphore_wait(barrier, SLOTS - 1 + 2 * (BLOCKS - 1))
+
+    for slot in range(1, 2 * NEAR):
+        place_copy(slot).start()
+    for block in range(BLOCKS - 1):
+        target_copy(block).start()
+    for slot in reversed(range(2 * NEAR, SLOTS)):
+        place_copy(slot).start()
+    start_density()
+    fem_copy().start()
+
+    for slot in range(1, 2 * NEAR):
+        place_copy(slot).wait_recv()
+
+    for slot in range(1, 2 * NEAR):
+        widen(slot)
+
+    for block in range(BLOCKS - 1):
+        target_copy(block).wait_recv()
+
+    @pl.loop(0, PAIRS)
+    def _(pair):
+        @pl.loop(0, NEAR)
+        def _(chunk):
+            tile_piece(pair, chunk)
+
+    for slot in range(2 * NEAR, SLOTS):
+        place_copy(slot).wait_recv()
+
+    @pl.loop(2 * NEAR, SLOTS, step=4)
+    def _(slot):
+        for i in range(4):
+            widen(slot + i)
 
     for slot in range(1, SLOTS):
-        place_copy(slot).wait()
-    for block in range(BLOCKS - 1):
-        target_copy(block).wait()
-
-    @pl.loop(0, SLOTS)
-    def _(slot):
-        columns = jnp.transpose(source_place[slot])
-        place = pl.ds(pl.multiple_of(slot * OWN, OWN), OWN)
-        for i in range(4):
-            wide = jnp.broadcast_to(columns[:, i : i + 1], (OWN, 128))
-            source_wide[i, place, :] = wide
-            if i == 3:
-                source_wide[4, place, :] = 1.5 * wide
-
-    @pl.loop(0, BLOCKS)
-    def _(block):
-        target = [
-            jnp.broadcast_to(target_place[block, i : i + 1, :], (16, OWN)) for i in range(3)
-        ]
-
-        @pl.loop(0, SOURCES // 128)
+        density_copy(0, slot).wait_recv()
+
+    for pair in range(PAIRS):
+
+        @pl.loop(NEAR, CHUNKS)
         def _(chunk):
-            for step in range(8):
-                place = pl.ds(pl.multiple_of(chunk * 128 + step * 16, 16), 16)
-                source = [source_wide[i, place, :] for i in range(5)]
-                values = kelvin_components(source, target)
-                for k in range(COMPONENTS):
-                    tile[k, block, place, :] = values[k].astype(BF16)
-
-    @pl.loop(0, SWEEPS)
+            tile_piece(pair, chunk)
+
+        blocks = (2 * pair, 2 * pair + 1)
+        accumulate(0, blocks, product(0, blocks, 0, CHUNKS), True)
+        send_partial(0, blocks)
+
+    next_density(0)
+
+    @pl.loop(1, SWEEPS)
     def _(sweep):
-        for slot in range(1, SLOTS):
-            density_copy(sweep, slot).wait_recv()
-        xy = jnp.concatenate([density[sweep, slot, 0:16, :] for slot in range(SLOTS)], axis=1)
-        zx = jnp.concatenate([density[sweep, slot, 16:32, :] for slot in range(SLOTS)], axis=1)
-        xyz = jnp.concatenate([xy, zx], axis=0)
-        for pair in range(0, BLOCKS, 2):
-
-            def product(left, k):
-                right = jnp.concatenate([tile[k, pair], tile[k, pair + 1]], axis=1)
-                return jnp.dot(left, right, preferred_element_type=F32)
-
-            p_xx = product(xy, 0)
-            p_xy = product(xy, 1)
-            p_xz = product(zx, 2)
-            p_yy = product(xy, 3)
-            p_yz = product(xyz, 4)
-            p_zz = product(zx, 5)
-            g_x = p_xx[0:8] + p_xy[8:16] + p_xz[0:8]
-            g_y = p_xy[0:8] + p_yy[8:16] + p_yz[16:24]
-            g_z = p_xz[8:16] + p_yz[8:16] + p_zz[0:8]
-            for block in (pair, pair + 1):
-                lanes = slice((block - pair) * OWN, (block - pair + 1) * OWN)
-                partial[sweep, block, 0] = g_x[:, lanes]
-                partial[sweep, block, 1] = g_y[:, lanes]
-                partial[sweep, block, 2] = g_z[:, lanes]
-                if block < BLOCKS - 1:
-                    partial_copy(sweep, block).start()
-        total = [partial[sweep, BLOCKS - 1, i] for i in range(3)]
-        for block in range(BLOCKS - 1):
-            partial_copy(sweep, block).wait_recv()
-            for i in range(3):
-                total[i] = total[i] + arrived[sweep, block, i]
+        for first, chunks in GROUPS:
+            for slot in range(max(1, 2 * first), 2 * (first + chunks)):
+                density_copy(sweep, slot).wait_recv()
+            if first + chunks < CHUNKS:
+                every = range(BLOCKS)
+                accumulate(sweep, every, product(sweep, every, first, chunks), first == 0)
+            else:
+                for pair in range(PAIRS):
+                    blocks = (2 * pair, 2 * pair + 1)
+                    accumulate(sweep, blocks, product(sweep, blocks, first, chunks), False)
+
+                    @pl.when(sweep == SWEEPS - 1)
+                    def _():
+                        for block in blocks:
+                            beside_copy(block).start()
+
+                    send_partial(sweep, blocks)
 
         @pl.when(sweep < SWEEPS - 1)
         def _():
-            stiffness = stiffness_ref[pl.ds(half, 1), :]
-            publish(sweep + 1, [trac[i] - stiffness * total[i] for i in range(3)])
-
-        @pl.when(sweep == SWEEPS - 1)
-        def _():
-            for i in range(3):
-                fem_wide = fem[i]
-                result[half, i] = fem_wide + RELAXATION * (total[i] - fem_wide)
-
-    exchange = pltpu.make_async_remote_copy(
-        src_ref=result.at[half],
-        dst_ref=result.at[half],
-        send_sem=result_send,
-        recv_sem=result_recv,
-        device_id=((half + 1) % 2, blk, rows),
-        device_id_type=MESH,
-    )
-    exchange.start()
+            next_density(sweep)
+
+    for slot in range(1, SLOTS):
+        place_copy(slot).wait_send()
+    for block in range(BLOCKS - 1):
+        target_copy(block).wait_send()
+    fem_copy().wait()
 
     @pl.loop(0, SWEEPS)
     def _(sweep):
@@ -400,9 +526,20 @@
         for block in range(BLOCKS - 1):
             partial_copy(sweep, block).wait_send()
 
-    exchange.wait()
+    own_total = total_of(SWEEPS - 1)
+    for block in range(BLOCKS):
+        beside_copy(block).wait_send()
+    other_total = [jnp.zeros((8, OWN), F32)] * 3
+    for block in reversed(range(BLOCKS)):
+        beside_copy(block).wait_recv()
+        for i in range(3):
+            other_total[i] = other_total[i] + beside[block, i]
     for i in range(3):
-        out_ref[i] = jnp.concatenate([result[0, i], result[1, i]], axis=1)
+        own_out = fem[0, i] + RELAXATION * (own_total[i] - fem[0, i])
+        other_out = fem[1, i] + RELAXATION * (other_total[i] - fem[1, i])
+        low = jnp.where(half == 0, own_out, other_out)
+        high = jnp.where(half == 0, other_out, own_out)
+        out_ref[i] = jnp.concatenate([low, high], axis=1)
 
 
 def on_device(
@@ -430,14 +567,22 @@
         for values in (brick_size, shear_modulus, bulk_modulus, cohesion, friction, active)
     ]
     by_node = [values.reshape(-1, OWN) for values in (patch_brick, patch_face)]
+    inputs = (
+        nodal_disp.transpose(1, 0, 2),
+        connect,
+        *by_brick,
+        *by_node,
+        coords,
+        radius.reshape(-1, OWN),
+        stiffness.reshape(-1, OWN),
+    )
     relaxed = pl.pallas_call(
         kernel,
         out_shape=jax.ShapeDtypeStruct((3, batches, local_nodes), F32),
-        in_specs=[anywhere] * 2 + [vmem] * 11,
+        in_specs=[anywhere] * len(inputs),
         out_specs=vmem,
         scratch_shapes=[
-            pltpu.VMEM((3, batches, nodal_disp.shape[2]), F32),
-            pltpu.VMEM(connect.shape, jnp.int32),
+            *(pltpu.VMEM(values.shape, values.dtype) for values in inputs),
             pltpu.VMEM((8, OWN), F32),
             pltpu.VMEM((SLOTS, 8, OWN), F32),
             pltpu.VMEM((BLOCKS, 8, OWN), F32),
@@ -447,9 +592,9 @@
             pltpu.VMEM((SWEEPS, BLOCKS, 3, 8, OWN), F32),
             pltpu.VMEM((SWEEPS, BLOCKS, 3, 8, OWN), F32),
             pltpu.VMEM((3, 8, OWN), F32),
-            pltpu.VMEM((3, 8, OWN), F32),
             pltpu.VMEM((2, 3, 8, OWN), F32),
-            dma((2,)),
+            pltpu.VMEM((BLOCKS, 3, 8, OWN), F32),
+            dma((len(inputs),)),
             dma((SLOTS,)),
             dma((SLOTS,)),
             dma((BLOCKS,)),
@@ -458,20 +603,16 @@
             dma((SWEEPS, SLOTS)),
             dma((SWEEPS, BLOCKS)),
             dma((SWEEPS, BLOCKS)),
+            dma((BLOCKS,)),
+            dma((BLOCKS,)),
             dma,
             dma,
         ],
         compiler_params=pltpu.CompilerParams(
-            collective_id=0, has_side_effects=True, vmem_limit_bytes=50 * 2**20
+            collective_id=0, has_side_effects=True, vmem_limit_bytes=60 * 2**20
         ),
     )(
-        nodal_disp.transpose(1, 0, 2),
-        connect,
-        *by_brick,
-        *by_node,
-        coords,
-        radius.reshape(-1, OWN),
-        stiffness.reshape(-1, OWN),
+        *inputs
     )
     return relaxed.transpose(1, 0, 2)
 

time: 67.4 us -> 53 us (0.79)
  local copies, waits for them, and re-layouts: 9.53 us -> 1.35 us
  Pallas kernels: 57.2 us -> 51.5 us
    unnamed x27 -> x1, local copies, waits for them, and re-layouts: 9.53 us -> 1.35 us
    pallas_call x1, Pallas kernels: 57.2 us -> 51.5 us  [on_device(): pl.pallas_call(kernel, out_shape=jax.ShapeDtypeStruct((3, batches, local_...]
where the time goes in v2:
time: 53 us; the launch traced here: 52.9 us
  Pallas kernels  51.5 us (97%)
  local copies, waits for them, and re-layouts  1.35 us (3%)
    pallas_call x1, Pallas kernels, on_device(): pl.pallas_call(kernel, out_shape=jax.ShapeDtypeStruct((3, batches, local_...  51.5 us
    unnamed x1, local copies, waits for them, and re-layouts  1.35 us

profile of v2, /device:TPU:1, one launch (start us, length us, event | category | flops | bytes accessed | tf_op | source)
XLA Modules:
  0.0 52.9 jit_solution(5498653999324090475)
XLA Ops:
  0.0 51.5 %shard_map.127 = f32[3,8,256]{2,1,0:T(8,128)} custom-call(f32[3,8,4096]{2,1,0:T(8,128)} %bitcast.12, s32[8,4096]{1,0:T(8,128)} %connect_hbm.1, f32[32,128]{1,0:T(8,128)} %bitcast.14, f32[32,128]{1,0:T(8,128)} %bitcast.15, f32[32,128]{1,0:T(8,128)} %bitcast.16, f32[32,128]{1,0:T(8,128)} %bitcast.17, f32[32,128]{1,0:T(8,128)} %bitcast.18, s32[32,128]{1,0:T(8,128)} %bitcast.19, ...), custom_call_target="tpu_custom_call" | custom-call | tf_op jit(solution)/shard_map/pallas_call | solution.py:579
  51.5 1.3 %copy.15 = f32[8,3,256]{2,0,1:T(8,128)} copy(f32[8,3,256]{2,0,1:T(8,128)} %bitcast.13) | data formatting | bytes 49152

commit v3 on v2

--- a/solution.py
+++ b/solution.py
@@ -199,6 +199,7 @@
     trac,
     fem,
     beside,
+    repeat,
     local_sem,
     place_send,
     place_recv,
@@ -232,6 +233,13 @@
     def beside_peer(block):
         _, _, peer_rows = target_peer(block)
         return ((half + 1) % 2, blk, peer_rows)
+
+    barrier = pltpu.get_barrier_semaphore()
+    peers = [source_peer(slot) for slot in reversed(range(1, SLOTS))]
+    peers[5:5] = [beside_peer(block) for block in range(BLOCKS - 1)]
+    peers += [target_peer(block) for block in range(BLOCKS - 1)]
+    for peer in peers:
+        pl.semaphore_signal(barrier, inc=1, device_id=peer, device_id_type=MESH)
 
     place_loads = [(coords_hbm, coords_ref), (radius_hbm, radius_ref)]
     brick_loads = [
@@ -254,20 +262,17 @@
     for load in loads:
         load.start()
 
-    barrier = pltpu.get_barrier_semaphore()
-    for slot in range(1, SLOTS):
-        pl.semaphore_signal(barrier, inc=1, device_id=source_peer(slot), device_id_type=MESH)
-    for block in range(BLOCKS - 1):
-        pl.semaphore_signal(barrier, inc=1, device_id=target_peer(block), device_id_type=MESH)
-        pl.semaphore_signal(barrier, inc=1, device_id=beside_peer(block), device_id_type=MESH)
-
     for load in loads[: len(place_loads)]:
         load.wait()
     own = pl.ds(pl.multiple_of(half * OWN, OWN), OWN)
     radius = radius_ref[pl.ds(half, 1), :]
     own_place[0:3, :] = coords_ref[:, own]
     own_place[3:4, :] = radius * radius
-    own_place[4:8, :] = jnp.zeros((4, OWN), F32)
+    own_place[4:5, :] = 1.5 * (radius * radius)
+    own_place[5:8, :] = jnp.zeros((3, OWN), F32)
+    row = lax.broadcasted_iota(jnp.int32, repeat.shape, 0)
+    column = lax.broadcasted_iota(jnp.int32, repeat.shape, 1)
+    repeat[...] = jnp.where((row % 8 == column // 128) & (row < 24), 1.0, 0.0).astype(BF16)
     source_place[0] = own_place[...]
     target_place[BLOCKS - 1] = own_place[...]
 
@@ -346,13 +351,21 @@
         return start
 
     def widen(slot):
-        columns = jnp.transpose(source_place[slot])
+        values = source_place[slot]
+        first = values.astype(BF16).astype(F32)
+        rest = values - first
+        second = rest.astype(BF16).astype(F32)
+        third = rest - second
+        parts = jnp.concatenate([first, second, third, jnp.zeros_like(third)], axis=0)
+        wide = lax.dot_general(
+            parts.astype(BF16),
+            repeat[...],
+            (((0,), (0,)), ((), ())),
+            preferred_element_type=F32,
+        )
         place = pl.ds(pl.multiple_of(slot * OWN, OWN), OWN)
-        for i in range(4):
-            wide = jnp.broadcast_to(columns[:, i : i + 1], (OWN, 128))
-            source_wide[i, place, :] = wide
-            if i == 3:
-                source_wide[4, place, :] = 1.5 * wide
+        for i in range(5):
+            source_wide[i, place, :] = wide[:, i * 128 : (i + 1) * 128]
 
     def tile_piece(pair, chunk):
         for block in (2 * pair, 2 * pair + 1):
@@ -360,15 +373,12 @@
                 jnp.broadcast_to(target_place[block, i : i + 1, :], (16, OWN)) for i in range(3)
             ]
 
-            @pl.loop(0, 2)
-            def _(part):
-                for step in range(8):
-                    first = chunk * 256 + part * 128 + step * 16
-                    place = pl.ds(pl.multiple_of(first, 16), 16)
-                    source = [source_wide[i, place, :] for i in range(5)]
-                    values = kelvin_components(source, target)
-                    for k in range(COMPONENTS):
-                        tile[k, block, place, :] = values[k].astype(BF16)
+            for step in range(16):
+                place = pl.ds(pl.multiple_of(chunk * 256 + step * 16, 16), 16)
+                source = [source_wide[i, place, :] for i in range(5)]
+                values = kelvin_components(source, target)
+                for k in range(COMPONENTS):
+                    tile[k, block, place, :] = values[k].astype(BF16)
 
     def product(sweep, blocks, chunk, chunks):
         slots = range(2 * chunks)
@@ -457,11 +467,11 @@
     for slot in range(1, 2 * NEAR):
         widen(slot)
 
-    for block in range(BLOCKS - 1):
-        target_copy(block).wait_recv()
-
-    @pl.loop(0, PAIRS)
-    def _(pair):
+    for pair in reversed(range(PAIRS)):
+        for block in (2 * pair, 2 * pair + 1):
+            if block < BLOCKS - 1:
+                target_copy(block).wait_recv()
+
         @pl.loop(0, NEAR)
         def _(chunk):
             tile_piece(pair, chunk)
@@ -469,9 +479,9 @@
     for slot in range(2 * NEAR, SLOTS):
         place_copy(slot).wait_recv()
 
-    @pl.loop(2 * NEAR, SLOTS, step=4)
+    @pl.loop(2 * NEAR, SLOTS, step=6)
     def _(slot):
-        for i in range(4):
+        for i in range(6):
             widen(slot + i)
 
     for slot in range(1, SLOTS):
@@ -594,6 +604,7 @@
             pltpu.VMEM((3, 8, OWN), F32),
             pltpu.VMEM((2, 3, 8, OWN), F32),
             pltpu.VMEM((BLOCKS, 3, 8, OWN), F32),
+            pltpu.VMEM((32, 5 * 128), BF16),
             dma((len(inputs),)),
             dma((SLOTS,)),
             dma((SLOTS,)),

time: 53 us -> 51.6 us (0.974)
  Pallas kernels: 51.5 us -> 50 us
    pallas_call x1, Pallas kernels: 51.5 us -> 50 us  [on_device(): pl.pallas_call(kernel, out_shape=jax.ShapeDtypeStruct((3, batches, local_...]
where the time goes in v3:
time: 51.6 us; the launch traced here: 51.4 us
  Pallas kernels  50 us (97%)
  local copies, waits for them, and re-layouts  1.35 us (3%)
    pallas_call x1, Pallas kernels, on_device(): pl.pallas_call(kernel, out_shape=jax.ShapeDtypeStruct((3, batches, local_...  50 us
    unnamed x1, local copies, waits for them, and re-layouts  1.35 us

profile of v3, /device:TPU:1, one launch (start us, length us, event | category | flops | bytes accessed | tf_op | source)
XLA Modules:
  0.0 51.4 jit_solution(7013595603050349547)
XLA Ops:
  0.0 50.0 %shard_map.127 = f32[3,8,256]{2,1,0:T(8,128)} custom-call(f32[3,8,4096]{2,1,0:T(8,128)} %bitcast.12, s32[8,4096]{1,0:T(8,128)} %connect_hbm.1, f32[32,128]{1,0:T(8,128)} %bitcast.14, f32[32,128]{1,0:T(8,128)} %bitcast.15, f32[32,128]{1,0:T(8,128)} %bitcast.16, f32[32,128]{1,0:T(8,128)} %bitcast.17, f32[32,128]{1,0:T(8,128)} %bitcast.18, s32[32,128]{1,0:T(8,128)} %bitcast.19, ...), custom_call_target="tpu_custom_call" | custom-call | tf_op jit(solution)/shard_map/pallas_call | solution.py:589
  50.1 1.3 %copy.15 = f32[8,3,256]{2,0,1:T(8,128)} copy(f32[8,3,256]{2,0,1:T(8,128)} %bitcast.13) | data formatting | bytes 49152

commit v4 on v3

--- a/solution.py
+++ b/solution.py
@@ -35,7 +35,7 @@
 PAIRS = BLOCKS // 2
 CHUNKS = SLOTS // 2
 NEAR = 2
-GROUPS = ((0, 2), (2, 6))
+EARLY = 2
 COMPONENTS = 6
 
 
@@ -501,23 +501,26 @@
 
     @pl.loop(1, SWEEPS)
     def _(sweep):
-        for first, chunks in GROUPS:
-            for slot in range(max(1, 2 * first), 2 * (first + chunks)):
-                density_copy(sweep, slot).wait_recv()
-            if first + chunks < CHUNKS:
-                every = range(BLOCKS)
-                accumulate(sweep, every, product(sweep, every, first, chunks), first == 0)
+        remote, near_pair = range(BLOCKS - 2), range(BLOCKS - 2, BLOCKS)
+        for slot in range(1, 2 * EARLY):
+            density_copy(sweep, slot).wait_recv()
+        accumulate(sweep, remote, product(sweep, remote, 0, EARLY), True)
+        for slot in range(2 * EARLY, SLOTS):
+            density_copy(sweep, slot).wait_recv()
+        for pair in range(PAIRS):
+            blocks = (2 * pair, 2 * pair + 1)
+            if pair < PAIRS - 1:
+                sums = product(sweep, blocks, EARLY, CHUNKS - EARLY)
+                accumulate(sweep, blocks, sums, False)
             else:
-                for pair in range(PAIRS):
-                    blocks = (2 * pair, 2 * pair + 1)
-                    accumulate(sweep, blocks, product(sweep, blocks, first, chunks), False)
-
-                    @pl.when(sweep == SWEEPS - 1)
-                    def _():
-                        for block in blocks:
-                            beside_copy(block).start()
-
-                    send_partial(sweep, blocks)
+                accumulate(sweep, blocks, product(sweep, blocks, 0, CHUNKS), True)
+
+            @pl.when(sweep == SWEEPS - 1)
+            def _():
+                for block in blocks:
+                    beside_copy(block).start()
+
+            send_partial(sweep, blocks)
 
         @pl.when(sweep < SWEEPS - 1)
         def _():

time: 51.6 us -> 51.1 us (level)
  no operation moved by 1% of the time
where the time goes in v4:
time: 51.1 us; the launch traced here: 51 us
  Pallas kernels  49.6 us (97%)
  local copies, waits for them, and re-layouts  1.35 us (3%)
    pallas_call x1, Pallas kernels, on_device(): pl.pallas_call(kernel, out_shape=jax.ShapeDtypeStruct((3, batches, local_...  49.6 us
    unnamed x1, local copies, waits for them, and re-layouts  1.35 us

profile of v4, /device:TPU:1, one launch (start us, length us, event | category | flops | bytes accessed | tf_op | source)
XLA Modules:
  0.0 51.0 jit_solution(4458785147720308853)
XLA Ops:
  0.0 49.6 %shard_map.127 = f32[3,8,256]{2,1,0:T(8,128)} custom-call(f32[3,8,4096]{2,1,0:T(8,128)} %bitcast.12, s32[8,4096]{1,0:T(8,128)} %connect_hbm.1, f32[32,128]{1,0:T(8,128)} %bitcast.14, f32[32,128]{1,0:T(8,128)} %bitcast.15, f32[32,128]{1,0:T(8,128)} %bitcast.16, f32[32,128]{1,0:T(8,128)} %bitcast.17, f32[32,128]{1,0:T(8,128)} %bitcast.18, s32[32,128]{1,0:T(8,128)} %bitcast.19, ...), custom_call_target="tpu_custom_call" | custom-call | tf_op jit(solution)/shard_map/pallas_call | solution.py:592
  49.6 1.3 %copy.15 = f32[8,3,256]{2,0,1:T(8,128)} copy(f32[8,3,256]{2,0,1:T(8,128)} %bitcast.13) | data formatting | bytes 49152

commit v5 on v4

--- a/solution.py
+++ b/solution.py
@@ -489,9 +489,10 @@
 
     for pair in range(PAIRS):
 
-        @pl.loop(NEAR, CHUNKS)
+        @pl.loop(NEAR, CHUNKS, step=2)
         def _(chunk):
             tile_piece(pair, chunk)
+            tile_piece(pair, chunk + 1)
 
         blocks = (2 * pair, 2 * pair + 1)
         accumulate(0, blocks, product(0, blocks, 0, CHUNKS), True)

time: 51.1 us -> 51.1 us (level)
  no operation moved by 1% of the time
where the time goes in v5:
time: 51.1 us; the launch traced here: 50.9 us
  Pallas kernels  49.5 us (97%)
  local copies, waits for them, and re-layouts  1.35 us (3%)
    pallas_call x1, Pallas kernels, on_device(): pl.pallas_call(kernel, out_shape=jax.ShapeDtypeStruct((3, batches, local_...  49.5 us
    unnamed x1, local copies, waits for them, and re-layouts  1.35 us

profile of v5, /device:TPU:1, one launch (start us, length us, event | category | flops | bytes accessed | tf_op | source)
XLA Modules:
  0.0 50.9 jit_solution(1136100180428743906)
XLA Ops:
  0.0 49.5 %shard_map.127 = f32[3,8,256]{2,1,0:T(8,128)} custom-call(f32[3,8,4096]{2,1,0:T(8,128)} %bitcast.12, s32[8,4096]{1,0:T(8,128)} %connect_hbm.1, f32[32,128]{1,0:T(8,128)} %bitcast.14, f32[32,128]{1,0:T(8,128)} %bitcast.15, f32[32,128]{1,0:T(8,128)} %bitcast.16, f32[32,128]{1,0:T(8,128)} %bitcast.17, f32[32,128]{1,0:T(8,128)} %bitcast.18, s32[32,128]{1,0:T(8,128)} %bitcast.19, ...), custom_call_target="tpu_custom_call" | custom-call | tf_op jit(solution)/shard_map/pallas_call | solution.py:593
  49.5 1.3 %copy.15 = f32[8,3,256]{2,0,1:T(8,128)} copy(f32[8,3,256]{2,0,1:T(8,128)} %bitcast.13) | data formatting | bytes 49152
